TPU v7x, 512 devices: a whole 4x4x16 slice. The times are simulated.
512 devices in a mesh: seq: 32 (over x, z_lo, core), head: 16 (over y, z_hi).
Axes of the slice: x: 4, y: 4, z: 16 (z_hi: 4, z_lo: 4; z = z_hi * 4 + z_lo), core: 2. Of those that a mesh axis runs over, the one named last changes fastest.
Arguments:
- tokens: bfloat16 [16384, 1152], P(('seq', 'head')), may hold values from -1.796875 to 1.796875
- qkv: bfloat16 [16384, 3456], P(('seq', 'head')), may hold values from -96 to 96, as said below
- out_weight: bfloat16 [1152, 1152], P(None, 'seq'), may hold values from -0.1875 to 0.1875
- out_bias: float32 [1152], replicated, may hold values from -1 to 1
- gate_table: bfloat16 [1000, 1152], replicated, may hold values from -5 to 5
- timesteps: int32 [4], replicated, may hold values from 0 to 999
- tile_mask: int32 [128, 128], replicated, may hold values from 0 to 1, as said below
Outputs:
- mixed: bfloat16 [16384, 1152], P(('seq', 'head'))
Inputs may be any that keep to these rules, and one draw needn't show every extreme that they name: `qkv`: columns are grouped by head: for each of the 16 heads its query, key and value, 72 columns each. `tile_mask`: A tile is 1 wherever the two tiles hold the same position within their frames (in any two frames). Otherwise a tile is 1 only where the two tiles' frames differ by at most one and their positions within their frames differ by at most 4 tiles.
All inputs are finite; a program needn't handle non-finite values.
Results may differ from a plain program's by a relative error of at most 0.009.
Values may be sent and summed in bfloat16 or wider, within the bound.
A program may use at most 128 MiB of HBM per device.

v0:
```python
import jax
import jax.numpy as jnp
from jax import lax
from jax.sharding import PartitionSpec as P

HEAD_DIM = 72
TILE = 128
FRAME = 4096
TSTEPS = 1000


def shards(tokens, qkv, out_weight, out_bias, gate_table, timesteps, tile_mask):
    n_head = lax.axis_size("head")
    tok_rows = tokens.shape[0]
    gathered = lax.all_to_all(qkv, "head", split_axis=1, concat_axis=0, tiled=True)
    rows = gathered.shape[0]
    local_heads = gathered.shape[1] // (3 * HEAD_DIM)
    grouped = gathered.reshape(rows, local_heads, 3, HEAD_DIM)
    query = grouped[:, :, 0]
    keys = grouped[:, :, 1]
    values = grouped[:, :, 2]
    scale = HEAD_DIM ** (-0.5)
    tile_count = tile_mask.shape[0]
    block_start = lax.axis_index("seq") * rows
    my_mask = lax.dynamic_slice_in_dim(tile_mask, block_start // TILE, rows // TILE, 0)
    key_piece = lax.all_gather(keys, "seq", axis=0, tiled=True)
    value_piece = lax.all_gather(values, "seq", axis=0, tiled=True)
    width = key_piece.shape[0]
    positions = jnp.arange(width)
    inside = (positions >= 0) & (positions < tile_count * TILE)
    key_tiles = jnp.clip(positions // TILE, 0, tile_count - 1)
    sub_mask = jnp.where(inside[None, :], jnp.take(my_mask, key_tiles, axis=1), 0)
    running = jnp.full((local_heads, rows), -1e30, jnp.float32)
    allowed = jnp.repeat(sub_mask, TILE, axis=0) > 0
    scores = (
        jnp.einsum("qhd,khd->hqk", query, key_piece, preferred_element_type=jnp.float32) * scale
    )
    scores = jnp.where(allowed[None], scores, -1e30)
    newest = jnp.maximum(running, jnp.max(scores, axis=-1))
    weights = jnp.where(allowed[None], jnp.exp(scores - newest[:, :, None]), 0.0)
    total = jnp.sum(weights, axis=-1)
    rounded = weights.astype(jnp.bfloat16)
    product = jnp.einsum("hqk,khd->hqd", rounded, value_piece, preferred_element_type=jnp.float32)
    summed = product
    running, total, summed = (newest, total, summed)
    attended = (summed / total[:, :, None]).astype(jnp.bfloat16)
    attended = jnp.transpose(attended, (1, 0, 2)).reshape(rows, local_heads * HEAD_DIM)
    restored = lax.all_to_all(attended, "head", split_axis=0, concat_axis=1, tiled=True)
    projected = jnp.dot(
        restored,
        lax.all_gather(out_weight, "seq", axis=1, tiled=True),
        preferred_element_type=jnp.float32,
    )
    first_token = (lax.axis_index("seq") * n_head + lax.axis_index("head")) * tok_rows
    frame_ids = (first_token + jnp.arange(tok_rows)) // FRAME
    chosen = jnp.take(timesteps, frame_ids)
    one_hot = (chosen[:, None] == jnp.arange(TSTEPS)[None, :]).astype(jnp.bfloat16)
    gate = jnp.dot(one_hot, gate_table, preferred_element_type=jnp.float32)
    mixed = tokens.astype(jnp.float32) + gate * (projected + out_bias)
    return mixed.astype(jnp.bfloat16)


def solution(mesh):
    return jax.shard_map(
        shards,
        mesh=mesh,
        in_specs=(
            P(("seq", "head"), None),
            P(("seq", "head"), None),
            P(None, "seq"),
            P(),
            P(),
            P(),
            P(),
        ),
        out_specs=P(("seq", "head"), None),
        check_vma=False,
    )
```

profile of v0, /device:TPU:1, one launch (start us, length us, event | category | flops | bytes accessed | tf_op | source)
XLA Modules:
  0.0 263.4 jit_solution(14240772500379605687)
XLA Ops:
  6.5 0.0 copy-start
  6.5 0.0 all-gather.7.cloned.1.call-start
  6.5 1.9 all_to_all.26
  8.4 0.1 copy.20
  8.5 38.0 %all_to_all.35 = bf16[32,16,216]{2,0,1:T(8,128)(2,1)S(1)} all-to-all(bf16[32,16,216]{2,0,1:T(8,128)(2,1)S(1)} %copy.20), channel_id=1, replica_groups=mesh['seq'=32,'head'=16] {'head'}, dimensions={1} | all-to-all | bytes 442368 | tf_op jit(solution)/shard_map/all_to_all | solution.py:15
  46.5 0.2 reshape.181
  46.8 1.3 fusion.26
  48.0 0.0 copy-start.3
  48.0 1.7 copy.22
  49.8 0.0 all-gather.7.cloned.1.call-update
  49.8 0.0 all-gather.9.cloned.1.call-start
  49.8 0.7 copy.23
  50.6 0.0 all-gather.9.cloned.1.call-update
  50.6 0.0 all-gather.11.cloned.1.call-start
  50.6 0.7 all-gather.11.cloned.1.call-update
  51.3 0.1 compare_select_fusion
  51.4 0.7 constant_dynamic-slice_fusion
  52.2 0.1 copy.26
  52.3 54.8 %gather_fusion = s32[16384,4]{1,0:T(8,128)} fusion(s32[4,128]{0,1:T(8,128)S(1)} %copy.26, s32[16384]{0:T(1024)S(1)} %broadcast_clamp_fusion), kind=kCustom, calls=%fused_computation | custom fusion | bytes 589824 | tf_op jit(solution)/shard_map/jit(_take)/gather | solution.py:32
  107.0 14.2 %fusion.3 = pred[4,16384]{0,1:T(8,128)(4,1)} fusion(s32[16384,4]{1,0:T(8,128)} %gather_fusion, pred[16384]{0:T(1024)(128)(4,1)S(1)} %get-tuple-element.16, pred[16384]{0:T(1024)(128)(4,1)S(1)} %get-tuple-element.17), kind=kLoop, calls=%fused_computation.7 | loop fusion | flops 196608 | bytes 360448 | tf_op jit(solution)/shard_map/gt | solution.py:34
  121.3 3.9 %copy.19 = pred[4,16384]{1,0:T(4,128)(4,1)S(1)} copy(pred[4,16384]{0,1:T(8,128)(4,1)} %fusion.3) | data formatting | bytes 131072 | tf_op jit(solution)/shard_map/gt | solution.py:34
  125.2 0.0 copy-done.3
  125.2 0.7 fusion.27
  125.9 2.6 and_select_fusion.2
  128.5 0.1 copy.21
  128.6 0.0 all-gather.7.cloned.1.call-done
  128.6 15.4 %fusion = (f32[512]{0:T(512)S(1)}, f32[512,16384]{1,0:T(8,128)}) fusion(pred[4,16384]{1,0:T(4,128)(4,1)S(1)} %copy.19, bf16[16384,1,1,72]{0,3,2,1:T(8,128)(2,1)} %all-gather.7.cloned.1.call-done, bf16[512,1,1,72]{0,3,2,1:T(8,128)(2,1)S(1)} %copy.21), kind=kOutput, calls=%fused_computation.3 | convolution fusion | flops 1233124864 | bytes 36055040 | tf_op jit(solution)/shard_map/qhd,khd->hqk/dot_general | solution.py:36
  144.1 22.5 %fusion.1 = (f32[512]{0:T(512)S(1)}, bf16[512,16384]{1,0:T(8,128)(2,1)}) fusion(f32[512,16384]{1,0:T(8,128)} %get-tuple-element.15, f32[512]{0:T(512)S(1)} %broadcast_maximum_fusion, pred[4,16384]{1,0:T(4,128)(4,1)S(1)} %copy.19), kind=kLoop, calls=%fused_computation.4 | loop fusion | flops 50331136 | bytes 50401280 | tf_op jit(solution)/shard_map/reduce_sum | solution.py:41
  166.6 10.3 %all-gather.9.cloned.1.call-done = bf16[16384,1,1,72]{0,3,2,1:T(8,128)(2,1)} async-done(((bf16[512,1,1,72]{0,3,2,1:T(8,128)(2,1)}), bf16[16384,1,1,72]{0,3,2,1:T(8,128)(2,1)}) %all-gather.9.cloned.1.call-update) | async-done | bytes 2359312 | tf_op jit(solution)/shard_map/all_gather | solution.py:27
  176.9 11.6 %fusion.14 = bf16[512,72]{0,1:T(8,128)(2,1)S(1)} fusion(bf16[512,16384]{1,0:T(8,128)(2,1)} %get-tuple-element.6, bf16[16384,1,1,72]{0,3,2,1:T(8,128)(2,1)} %all-gather.9.cloned.1.call-done, f32[512]{0:T(512)S(1)} %get-tuple-element.5), kind=kOutput, calls=%fused_computation.17 | convolution fusion | flops 1208033280 | bytes 19212288 | tf_op jit(solution)/shard_map/hqk,khd->hqd/dot_general | solution.py:43
  188.5 0.0 copy-start.1
  188.5 0.0 copy-start.2
  188.5 0.7 copy.24
  189.3 12.9 %all-to-all-start.1 = ((bf16[16,32,72]{2,1,0:T(8,128)(2,1)}), bf16[16,32,72]{2,1,0:T(8,128)(2,1)S(1)}, u32[]{:S(2)}, u32[]{:S(2)}) async-start(bf16[16,32,72]{2,1,0:T(8,128)(2,1)} %bitcast.12), calls=%async_computation.1 | async-start | bytes 262144 | tf_op jit(solution)/shard_map/all_to_all | solution.py:48
  202.2 0.0 copy-done
  202.2 0.5 fusion.17
  202.8 45.3 %all-gather.11.cloned.1.call-done = bf16[32,36,1152]{2,1,0:T(8,128)(2,1)} async-done(((bf16[1,36,1152]{2,1,0:T(8,128)(2,1)}), bf16[32,36,1152]{2,1,0:T(8,128)(2,1)}) %all-gather.11.cloned.1.call-update) | async-done | bytes 2654224 | tf_op jit(solution)/shard_map/all_gather | solution.py:51
  248.1 5.2 %reshape.222 = bf16[1152,1152]{1,0:T(8,128)(2,1)} reshape(bf16[32,36,1152]{2,1,0:T(8,128)(2,1)} %all-gather.11.cloned.1.call-done) | data formatting | bytes 5308416
  253.3 0.0 all-to-all-done.1
  253.3 0.1 copy.25
  253.4 0.2 all_to_all.32
  253.5 0.0 copy-done.1
  253.6 0.0 copy-done.2
  253.6 3.3 %fusion.10 = bf16[32,1152]{1,0:T(8,128)(2,1)} fusion(f32[32,1152]{1,0:T(8,128)S(1)} %fusion.17, bf16[32,1152]{1,0:T(8,128)(2,1)S(1)} %all_to_all.32, bf16[1152,1152]{1,0:T(8,128)(2,1)} %reshape.222, bf16[32,1152]{1,0:T(8,128)(2,1)S(1)} %copy-done.1, f32[1152]{0:T(1024)S(1)} %copy-done.2), kind=kOutput, calls=%fused_computation.15 | convolution fusion | flops 85118976 | bytes 3027456 | tf_op jit(solution)/shard_map/dot_general | solution.py:49
  (3 shorter events, 0.0 us)
Async XLA Ops:
  6.5 195.7 %copy-start = (bf16[1000,1152]{1,0:T(8,128)(2,1)S(1)}, bf16[1000,1152]{1,0:T(8,128)(2,1)}, u32[]{:S(2)}) copy-start(bf16[1000,1152]{1,0:T(8,128)(2,1)} %param.11) | copy-start | bytes 6912004
  6.5 122.1 %all-gather.7.cloned.1.call-start = ((), (), s32[]{:S(2)}) async-start(), calls=%async_computation.2 | async-start | bytes 2433024 | tf_op jit(solution)/shard_map/all_gather | solution.py:26
  48.0 77.2 %copy-start.3 = (s32[4]{0:T(128)S(1)}, s32[4]{0:T(128)}, u32[]{:S(2)}) copy-start(s32[4]{0:T(128)} %param.12) | copy-start | bytes 52
  49.8 127.1 %all-gather.9.cloned.1.call-start = ((), (), s32[]{:S(2)}) async-start(), calls=%async_computation.3 | async-start | bytes 2433024 | tf_op jit(solution)/shard_map/all_gather | solution.py:27
  50.6 197.5 %all-gather.11.cloned.1.call-start = ((), (), s32[]{:S(2)}) async-start(), calls=%async_computation.4 | async-start | bytes 3041280 | tf_op jit(solution)/shard_map/all_gather | solution.py:51
  188.5 65.0 %copy-start.1 = (bf16[32,1152]{1,0:T(8,128)(2,1)S(1)}, bf16[32,1152]{1,0:T(8,128)(2,1)}, u32[]{:S(2)}) copy-start(bf16[32,1152]{1,0:T(8,128)(2,1)} %param.7) | copy-start | bytes 221188
  188.5 65.0 %copy-start.2 = (f32[1152]{0:T(1024)S(1)}, f32[1152]{0:T(1024)}, u32[]{:S(2)}) copy-start(f32[1152]{0:T(1024)} %param.10) | copy-start | bytes 13828
  189.3 64.0 %all-to-all-start.1 = ((bf16[16,32,72]{2,1,0:T(8,128)(2,1)}), bf16[16,32,72]{2,1,0:T(8,128)(2,1)S(1)}, u32[]{:S(2)}, u32[]{:S(2)}) async-start(bf16[16,32,72]{2,1,0:T(8,128)(2,1)} %bitcast.12), calls=%async_computation.1 | async-start | bytes 262144 | tf_op jit(solution)/shard_map/all_to_all | solution.py:48
Sparse Core Ops, SparseCore 0:
  49.9 60.0 all-gather.6
  112.1 64.7 all-gather.8
  179.0 69.0 all-gather.10
where the time goes:
time: 264 us; the launch traced here: 263 us
  local copies, waits for them, and re-layouts  72.4 us (27%)
  waiting for transfers between devices  56.4 us (21%)
  other arithmetic  39.4 us (15%)
  blocking collectives  38 us (14%)
  matrix products  30.9 us (12%)
  between operations  13.3 us (5%)
  starting transfers between devices  13 us (5%)
    gather x1, local copies, waits for them, and re-layouts, shards(): jnp.take(my_mask, key_tiles, axis=1)  54.8 us
    all_gather x1, waiting for transfers between devices, shards(): lax.all_gather(out_weight, 'seq', axis=1, tiled=True)  45.3 us
    all_to_all x1, blocking collectives, shards(): lax.all_to_all(qkv, 'head', split_axis=1, concat_axis=0, tiled=True)  38 us
    reduce_sum x1, other arithmetic, shards(): total = jnp.sum(weights, axis=-1)  22.5 us
    dot_general x1, matrix products, shards(): jnp.einsum('qhd,khd->hqk', query, key_piece, preferred_element_type=jnp.f...  15.4 us
    gt x1, other arithmetic, shards(): allowed = jnp.repeat(sub_mask, TILE, axis=0) > 0  14.2 us
    all_to_all x1, starting transfers between devices, shards(): lax.all_to_all(attended, 'head', split_axis=0, concat_axis=1, tiled=True)  12.9 us
    dot_general x1, matrix products, shards(): jnp.einsum('hqk,khd->hqd', rounded, value_piece, preferred_element_type=j...  11.6 us
  transfers between devices with their start and end apart: 4, of which 2 were waited for; matrix products, arithmetic and copies ran while one was open for 51% of the time, Pallas kernels for 0%

commit v1 on v0

v1 whole, which is shorter than its diff:
```python
import functools
import math

import jax
import jax.numpy as jnp
from jax import lax
from jax.experimental import pallas as pl
from jax.experimental.pallas import tpu as pltpu
from jax.sharding import PartitionSpec as P

F32 = jnp.float32
BF16 = jnp.bfloat16
MESH = pl.DeviceIdType.MESH

HD = 72
TILE = 128
BLOCK = 512
KV = 2 * HD
KVR = KV + 16
GROUP = 4 * 3 * HD
GPAD = 896
COLS = 36
FAR = 1e30
C_EXP = HD ** (-0.5) * math.log2(math.e)

Z0, YK0, YQ0, X0, P0, WX0, WZ0, WC0, B0, R0, NSEM = 0, 3, 6, 9, 12, 18, 21, 24, 25, 28, 31


def body(tok_ref, qkv_ref, w_ref, bias_ref, gate_hbm, ts_ref, mask_ref, out_ref,
         zsend, zrecv, zt, ykv, yq, qbuf, qs, kvbuf, acc, mrun, bsend, brecv,
         wf, wtmp, wall, wfull, wt, psend, precv, gate_v, gate_row, send_sem, recv_sem, gate_sem):
    seq = lax.axis_index("seq")
    head = lax.axis_index("head")
    x = seq // 8
    p = lax.rem(seq, 8)
    zl = p // 2
    c = lax.rem(p, 2)
    y = head // 4
    zh = lax.rem(head, 4)
    z = zh * 4 + zl

    def at_z(new_z, core):
        nz = lax.rem(new_z + 16, 16)
        return (x * 8 + lax.rem(nz, 4) * 2 + core, y * 4 + nz // 4)

    def zpeer(d):
        return (seq, y * 4 + lax.rem(zh + d, 4))

    def ypeer(d):
        return (seq, lax.rem(y + d, 4) * 4 + zh)

    def xpeer(d):
        return (lax.rem(x + d, 4) * 8 + p, head)

    def remote(src, dst, k, dev):
        return pltpu.make_async_remote_copy(
            src_ref=src, dst_ref=dst, send_sem=send_sem.at[k], recv_sem=recv_sem.at[k],
            device_id=dev, device_id_type=MESH)

    barrier = pltpu.get_barrier_semaphore()
    far_z = jnp.where(c == 0, z + 2, z + 14)
    from_z = jnp.where(c == 0, z + 14, z + 2)
    peers = [f(d) for f in (zpeer, ypeer, xpeer) for d in (1, 2, 3)]
    peers += [at_z(z + 1, c), at_z(z + 15, c), at_z(far_z, c), at_z(from_z, c)]
    for dev in peers:
        pl.semaphore_signal(barrier, inc=1, device_id=dev, device_id_type=MESH)

    @pl.when(p > 0)
    def _():
        pl.semaphore_signal(barrier, inc=1, device_id=(seq - 1, head), device_id_type=MESH)

    @pl.when(p < 7)
    def _():
        pl.semaphore_signal(barrier, inc=1, device_id=(seq + 1, head), device_id_type=MESH)

    gate_copy = pltpu.make_async_copy(gate_hbm, gate_v, gate_sem.at[0])
    gate_copy.start()

    for g in range(4):
        first = (GROUP * g) // TILE
        off = GROUP * g - first * TILE
        tiles = -(-(off + GROUP) // TILE)
        piece = qkv_ref[:, first * TILE:(first + tiles) * TILE].astype(F32)
        if off:
            piece = pltpu.roll(piece, tiles * TILE - off, 1)
        zsend[g] = piece[:, :GPAD].astype(BF16)

    count = 13 + jnp.where(p > 0, 1, 0) + jnp.where(p < 7, 1, 0)
    pl.semaphore_wait(barrier, count)

    zcopies = []
    for d in (2, 1, 3):
        zc = remote(zsend.at[lax.rem(zh + d, 4)], zrecv.at[zh], Z0 + d - 1, zpeer(d))
        zc.start()
        zcopies.append(zc)
    zrecv[zh] = zsend[zh]

    wf[...] = jnp.zeros_like(wf)
    wf[:, 0:COLS] = w_ref[...].astype(F32)
    wtmp[...] = jnp.zeros_like(wtmp)
    for g in range(4):
        row = pl.multiple_of((g * 4 + y) * HD, 8)
        wtmp[80 * g:80 * g + HD, :] = wf[pl.ds(row, HD), :]
    for j in range(3):
        wall[c, zl, x, :, TILE * j:TILE * (j + 1)] = (
            jnp.transpose(wtmp[TILE * j:TILE * (j + 1), :])[0:48].astype(BF16))
    wx = [remote(wall.at[c, zl, x], wall.at[c, zl, x], WX0 + d - 1, xpeer(d)) for d in (1, 2, 3)]
    for w in wx:
        w.start()

    for f in range(4):
        kvbuf[f, KV:KVR, :] = jnp.ones((KVR - KV, 3 * BLOCK), BF16)

    @pl.when(p == 0)
    def _():
        for f in range(4):
            kvbuf[f, 0:KV, 0:BLOCK] = jnp.zeros((KV, BLOCK), BF16)

    @pl.when(p == 7)
    def _():
        for f in range(4):
            kvbuf[f, 0:KV, 2 * BLOCK:3 * BLOCK] = jnp.zeros((KV, BLOCK), BF16)

    gate_copy.wait()
    step = ts_ref[x]
    one_hot = (lax.broadcasted_iota(jnp.int32, (16, 1000), 1) == step).astype(F32).astype(BF16)
    gate_row[...] = jnp.dot(one_hot, gate_v[...], preferred_element_type=F32)

    for zc in zcopies:
        zc.wait()

    for j in range(GPAD // TILE):
        part = zrecv[:, :, TILE * j:TILE * (j + 1)].reshape(TILE, TILE).astype(F32)
        zt[TILE * j:TILE * (j + 1), :] = jnp.transpose(part)
    for g in range(4):
        ykv[g] = zt[3 * HD * g + HD:3 * HD * (g + 1), :].astype(BF16)
        yq[g] = jnp.concatenate(
            [zt[3 * HD * g:3 * HD * g + HD, :], jnp.zeros((8, TILE), F32)], axis=0).astype(BF16)
    own_lane = pl.multiple_of(BLOCK + y * TILE, TILE)
    ycopies = []
    for d in (2, 1, 3):
        dest = lax.rem(y + d, 4)
        yc = remote(ykv.at[dest], kvbuf.at[x, 0:KV, pl.ds(own_lane, TILE)], YK0 + d - 1, ypeer(d))
        yc.start()
        ycopies.append(yc)
    for d in (2, 1, 3):
        dest = lax.rem(y + d, 4)
        yc = remote(yq.at[dest], qbuf.at[y], YQ0 + d - 1, ypeer(d))
        yc.start()
        ycopies.append(yc)
    kvbuf[x, 0:KV, pl.ds(own_lane, TILE)] = ykv[y]
    qbuf[y] = yq[y]

    for w in wx:
        w.wait()
    group = wall.at[c, zl]
    wz = [remote(group, group, WZ0, at_z(z + 1, c)),
          remote(group, group, WZ0 + 1, at_z(z + 15, c)),
          remote(group, group, WZ0 + 2, at_z(far_z, c))]
    for w in wz:
        w.start()

    for yc in ycopies[:3]:
        yc.wait()

    center = kvbuf.at[x, 0:KV, BLOCK:2 * BLOCK]
    xcopies = {d: remote(center, center, X0 + d - 1, xpeer(d)) for d in (1, 2, 3)}
    for d in (1, 3, 2):
        xcopies[d].start()

    def side_copy(side, rel, frame):
        src = kvbuf.at[frame, 0:KV, BLOCK:2 * BLOCK]
        if side == 0:
            return remote(src, kvbuf.at[frame, 0:KV, 0:BLOCK], P0 + rel, (seq + 1, head))
        return remote(src, kvbuf.at[frame, 0:KV, 2 * BLOCK:3 * BLOCK], P0 + 3 + rel, (seq - 1, head))

    frames = (x, x - 1, x + 1)
    lives = (x >= 0, x > 0, x < 3)

    def sides(rel, what):
        live = lives[rel]
        up, down = p < 7, p > 0
        for side in (0, 1):
            sends, gets = (up, down) if side == 0 else (down, up)

            @pl.when(live & (gets if what == "recv" else sends))
            def _():
                copy = side_copy(side, rel, frames[rel])
                if what == "start":
                    copy.start()
                elif what == "recv":
                    copy.wait_recv()
                else:
                    copy.wait_send()

    sides(0, "start")
    for yc in ycopies[3:]:
        yc.wait()
    for a in range(4):
        padded = jnp.concatenate([qbuf[a].astype(F32), jnp.zeros((48, TILE), F32)], axis=0)
        qs[a] = jnp.transpose(padded).astype(BF16)

    def attend(frame, tiles, first):
        @pl.loop(0, 4)
        def _(a):
            lead = 4 if tiles == 9 else 0
            base = a + 4 - lead
            lanes = pl.ds(pl.multiple_of(base * TILE, TILE), tiles * TILE)
            q = qs[a]
            s = jnp.dot(q, kvbuf[frame, 0:TILE, lanes], preferred_element_type=F32)
            top = None
            pens = []
            for t in range(tiles):
                spot = 4 * p + a - lead + t
                inside = (spot >= 0) & (spot < 32)
                live = mask_ref[4 * seq + a, frame * 32 + jnp.clip(spot, 0, 31)]
                pen = jnp.where(inside, jnp.where(live > 0, 0.0, FAR), FAR).astype(F32)
                pens.append(pen)
                val = s[:, t * TILE:(t + 1) * TILE] - pen
                top = val if top is None else jnp.maximum(top, val)
            m = jnp.max(top, axis=1, keepdims=True)
            if not first:
                old = mrun[a][:, 0:1]
                m = jnp.maximum(m, old)
            mc = m * C_EXP
            weights = jnp.concatenate(
                [jnp.exp2(s[:, t * TILE:(t + 1) * TILE] * C_EXP - (mc + pens[t])).astype(BF16)
                 for t in range(tiles)], axis=1)
            got = lax.dot_general(weights, kvbuf[frame, :, lanes], (((1,), (1,)), ((), ())),
                                  preferred_element_type=F32)
            if first:
                acc[a, :, 0:KVR] = got
            else:
                acc[a, :, 0:KVR] = acc[a, :, 0:KVR] * jnp.exp2((old - m) * C_EXP) + got
            mrun[a] = jnp.broadcast_to(m, (TILE, TILE))

    sides(0, "recv")
    attend(x, 9, True)
    xcopies[1].wait_recv()
    sides(1, "start")
    xcopies[3].wait_recv()
    sides(2, "start")
    for w in wz:
        w.wait()
    wc = remote(wall.at[c], wall.at[c], WC0, (seq + 1 - 2 * c, head))
    wc.start()
    xcopies[2].wait_recv()
    attend(lax.rem(x + 2, 4), 1, False)
    sides(1, "recv")

    @pl.when(x > 0)
    def _():
        attend(x - 1, 9, False)

    @pl.when(x == 0)
    def _():
        attend(3, 1, False)

    sides(2, "recv")

    @pl.when(x < 3)
    def _():
        attend(x + 1, 9, False)

    @pl.when(x == 3)
    def _():
        attend(0, 1, False)

    bcopies = []
    for g in range(4):
        rows = acc[:, 32 * g:32 * (g + 1), :].reshape(TILE, 2 * TILE)
        low = jnp.transpose(rows[:, 0:TILE])
        high = jnp.transpose(rows[:, TILE:2 * TILE])
        total = high[KV - TILE:KV - TILE + 1]
        feats = jnp.concatenate([low[HD:TILE], high[0:KV - TILE]], axis=0) / total
        bsend[g] = jnp.concatenate([feats, jnp.zeros((8, TILE), F32)], axis=0).astype(BF16)
    for d in (2, 1, 3):
        bc = remote(bsend.at[lax.rem(zh + d, 4)], brecv.at[zh], B0 + d - 1, zpeer(d))
        bc.start()
        bcopies.append(bc)
    brecv[zh] = bsend[zh]

    wc.wait()
    for s in range(32):
        piece = wall[s % 2, (s % 8) // 2, s // 8]
        wfull[COLS * s:COLS * (s + 1), :] = piece[0:COLS].astype(F32)
    wt[...] = wfull[...].astype(BF16)

    for bc in bcopies:
        bc.wait()
    feats = jnp.concatenate(
        [brecv[...].reshape(320, TILE).astype(F32), jnp.zeros((64, TILE), F32)], axis=0)
    att = jnp.concatenate(
        [jnp.transpose(feats[TILE * j:TILE * (j + 1)]) for j in range(3)], axis=1).astype(BF16)
    acc2 = lax.dot_general(att, wt[...], (((1,), (1,)), ((), ())), preferred_element_type=F32)
    psum = acc2
    for g in range(4):
        psend[g] = psum[32 * g:32 * (g + 1)].astype(BF16)
    rcopies = []
    for d in (2, 1, 3):
        rc = remote(psend.at[lax.rem(y + d, 4)], precv.at[d - 1], R0 + d - 1, ypeer(d))
        rc.start()
        rcopies.append(rc)
    own = jnp.where(y == 0, psum[0:32], jnp.where(y == 1, psum[32:64], jnp.where(y == 2, psum[64:96], psum[96:128])))
    own = own + bias_ref[...]
    for rc in rcopies:
        rc.wait()
    proj = own + precv[0].astype(F32) + precv[1].astype(F32) + precv[2].astype(F32)
    out_ref[...] = (tok_ref[...].astype(F32) + gate_row[0:1, :] * proj).astype(BF16)

    for d in (1, 2, 3):
        xcopies[d].wait_send()
    for rel in range(3):
        sides(rel, "send")


def shards(tokens, qkv, out_weight, out_bias, gate_table, timesteps, tile_mask):
    d = tokens.shape[1]
    vm = pl.BlockSpec(memory_space=pltpu.VMEM)
    sm = pl.BlockSpec(memory_space=pltpu.SMEM)
    return pl.pallas_call(
        body,
        out_shape=jax.ShapeDtypeStruct(tokens.shape, BF16),
        in_specs=[vm, vm, vm, vm, pl.BlockSpec(memory_space=pl.ANY), sm, sm],
        out_specs=vm,
        scratch_shapes=[
            pltpu.VMEM((4, 32, GPAD), BF16),
            pltpu.VMEM((4, 32, GPAD), BF16),
            pltpu.VMEM((GPAD, TILE), F32),
            pltpu.VMEM((4, KV, TILE), BF16),
            pltpu.VMEM((4, 80, TILE), BF16),
            pltpu.VMEM((4, 80, TILE), BF16),
            pltpu.VMEM((4, TILE, TILE), BF16),
            pltpu.VMEM((4, KVR, 3 * BLOCK), BF16),
            pltpu.VMEM((4, TILE, 2 * TILE), F32),
            pltpu.VMEM((4, TILE, TILE), F32),
            pltpu.VMEM((4, 80, TILE), BF16),
            pltpu.VMEM((4, 80, TILE), BF16),
            pltpu.VMEM((d, TILE), F32),
            pltpu.VMEM((384, TILE), F32),
            pltpu.VMEM((2, 4, 4, 48, 384), BF16),
            pltpu.VMEM((d, 384), F32),
            pltpu.VMEM((d, 384), BF16),
            pltpu.VMEM((4, 32, d), BF16),
            pltpu.VMEM((3, 32, d), BF16),
            pltpu.VMEM(gate_table.shape, BF16),
            pltpu.VMEM((16, d), F32),
            pltpu.SemaphoreType.DMA((NSEM,)),
            pltpu.SemaphoreType.DMA((NSEM,)),
            pltpu.SemaphoreType.DMA((1,)),
        ],
        compiler_params=pltpu.CompilerParams(
            collective_id=0, has_side_effects=True, vmem_limit_bytes=40 * 1024 * 1024),
    )(tokens, qkv, out_weight, out_bias.reshape(1, d), gate_table, timesteps, tile_mask)


def solution(mesh):
    return jax.shard_map(
        shards,
        mesh=mesh,
        in_specs=(
            P(("seq", "head"), None),
            P(("seq", "head"), None),
            P(None, "seq"),
            P(),
            P(),
            P(),
            P(),
        ),
        out_specs=P(("seq", "head"), None),
        check_vma=False,
    )
```

time: 264 us -> 72.6 us (0.27)
  the two profiles are of different devices: /device:TPU:1 before, /device:TPU:67 now
where the time goes in v1:
time: 72.6 us; the launch traced here: 72.3 us
  Pallas kernels  64.8 us (89%)
  local copies, waits for them, and re-layouts  7.43 us (10%)
    pallas_call x1, Pallas kernels, shards(): pl.pallas_call(body, out_shape=jax.ShapeDtypeStruct(tokens.shape, BF16),...  64.8 us
    unnamed x12, local copies, waits for them, and re-layouts  6.73 us

profile of v1, /device:TPU:67, one launch (start us, length us, event | category | flops | bytes accessed | tf_op | source)
XLA Modules:
  0.0 72.3 jit_solution(7276379099437178815)
XLA Ops:
  0.0 0.7 reshape.3.bias_ref
  0.7 1.1 %copy.8.w_ref = bf16[1152,36]{1,0:T(8,128)(2,1)S(1)} copy(bf16[1152,36]{0,1:T(8,128)(2,1)} %param.9) | data formatting | bytes 165888 | tf_op args[2]
  1.8 0.0 copy-start
  1.8 1.7 %copy-done = bf16[1000,1152]{1,0:T(8,128)(2,1)S(1)} copy-done((bf16[1000,1152]{1,0:T(8,128)(2,1)S(1)}, bf16[1000,1152]{1,0:T(8,128)(2,1)}, u32[]{:S(2)}) %copy-start) | copy-done | bytes 2304024
  3.5 0.0 copy-start.1
  3.5 0.9 %copy-done.1 = bf16[32,3456]{1,0:T(8,128)(2,1)S(1)} copy-done((bf16[32,3456]{1,0:T(8,128)(2,1)S(1)}, bf16[32,3456]{1,0:T(8,128)(2,1)}, u32[]{:S(2)}) %copy-start.1) | copy-done | bytes 221208
  4.4 0.0 copy-start.2
  4.4 0.9 %copy-done.2 = bf16[32,1152]{1,0:T(8,128)(2,1)S(1)} copy-done((bf16[32,1152]{1,0:T(8,128)(2,1)S(1)}, bf16[32,1152]{1,0:T(8,128)(2,1)}, u32[]{:S(2)}) %copy-start.2) | copy-done | bytes 73752
  5.3 0.0 copy-start.3
  5.3 0.8 %copy-done.3 = s32[128,128]{1,0:T(8,128)S(1)} copy-done((s32[128,128]{1,0:T(8,128)S(1)}, s32[128,128]{1,0:T(8,128)}, u32[]{:S(2)}) %copy-start.3) | copy-done | bytes 65560
  6.2 0.0 copy-start.4
  6.2 0.7 copy-done.4
  6.8 64.8 %shard_map.73 = bf16[32,1152]{1,0:T(8,128)(2,1)S(1)} custom-call(bf16[32,1152]{1,0:T(8,128)(2,1)S(1)} %copy-done.2, bf16[32,3456]{1,0:T(8,128)(2,1)S(1)} %copy-done.1, bf16[1152,36]{1,0:T(8,128)(2,1)S(1)} %copy.8.w_ref, f32[1,1152]{1,0:T(1,128)S(1)} %reshape.3.bias_ref, bf16[1000,1152]{1,0:T(8,128)(2,1)S(1)} %copy-done, s32[4]{0:T(128)S(1)} %copy-done.4, ...), custom_call_target="tpu_custom_call" | custom-call | tf_op jit(solution)/shard_map/pallas_call | solution.py:321
  71.6 0.6 copy.10
Async XLA Ops:
  1.8 1.7 %copy-start = (bf16[1000,1152]{1,0:T(8,128)(2,1)S(1)}, bf16[1000,1152]{1,0:T(8,128)(2,1)}, u32[]{:S(2)}) copy-start(bf16[1000,1152]{1,0:T(8,128)(2,1)} %gate_hbm.1) | copy-start | bytes 6912004
  3.5 0.9 %copy-start.1 = (bf16[32,3456]{1,0:T(8,128)(2,1)S(1)}, bf16[32,3456]{1,0:T(8,128)(2,1)}, u32[]{:S(2)}) copy-start(bf16[32,3456]{1,0:T(8,128)(2,1)} %qkv_ref.1) | copy-start | bytes 663556
  4.4 0.9 %copy-start.2 = (bf16[32,1152]{1,0:T(8,128)(2,1)S(1)}, bf16[32,1152]{1,0:T(8,128)(2,1)}, u32[]{:S(2)}) copy-start(bf16[32,1152]{1,0:T(8,128)(2,1)} %tok_ref.1) | copy-start | bytes 221188
  5.3 0.8 %copy-start.3 = (s32[128,128]{1,0:T(8,128)S(1)}, s32[128,128]{1,0:T(8,128)}, u32[]{:S(2)}) copy-start(s32[128,128]{1,0:T(8,128)} %mask_ref.1) | copy-start | bytes 196612
  6.2 0.7 copy-start.4

commit v2 on v1

v2 whole, which is shorter than its diff:
```python
import functools
import math

import jax
import jax.numpy as jnp
from jax import lax
from jax.experimental import pallas as pl
from jax.experimental.pallas import tpu as pltpu
from jax.sharding import PartitionSpec as P

F32 = jnp.float32
BF16 = jnp.bfloat16
MESH = pl.DeviceIdType.MESH

HD = 72
TILE = 128
BLOCK = 512
KV = 2 * HD
KVR = KV + 16
GROUP = 4 * 3 * HD
GPAD = 896
CUT = 640
COLS = 36
FAR = 1e30
C_EXP = HD ** (-0.5) * math.log2(math.e)

ZA, ZB, YK, YQ, X0, PO, PF, WZ, WX, WC, B0, R0, NSEM = 0, 3, 6, 9, 12, 24, 26, 42, 45, 48, 52, 55, 64
ORDER = (1, 3, 2)


def body(tok_hbm, qkv_hbm, w_hbm, bias_hbm, gate_hbm, ts_hbm, mask_hbm, out_ref,
         tok_ref, qkv_ref, w_ref, bias_ref, ts_ref, mask_ref, zsa, zsb, zra, zrb, zt, ykv, yq, qbuf, qs,
         kvbuf, acc, mrun, bsend, brecv, wf, wall, wfull, wt, part, psend, precv, gate_v, gate_row,
         send_sem, recv_sem, in_sem):
    seq = lax.axis_index("seq")
    head = lax.axis_index("head")
    x = seq // 8
    p = lax.rem(seq, 8)
    zl = p // 2
    c = lax.rem(p, 2)
    y = head // 4
    zh = lax.rem(head, 4)
    z = zh * 4 + zl

    def at_z(new_z, core):
        nz = lax.rem(new_z + 16, 16)
        return (x * 8 + lax.rem(nz, 4) * 2 + core, y * 4 + nz // 4)

    def zpeer(d):
        return (seq, y * 4 + lax.rem(zh + d, 4))

    def ypeer(d):
        return (seq, lax.rem(y + d, 4) * 4 + zh)

    def xpeer(d):
        return (lax.rem(x + d, 4) * 8 + p, head)

    def remote(src, dst, k, dev):
        return pltpu.make_async_remote_copy(
            src_ref=src, dst_ref=dst, send_sem=send_sem.at[k], recv_sem=recv_sem.at[k],
            device_id=dev, device_id_type=MESH)

    mask_row = pl.multiple_of((seq // 2) * 8, 8)
    loads = [pltpu.make_async_copy(src, dst, in_sem.at[k]) for k, (src, dst) in enumerate((
        (qkv_hbm, qkv_ref), (w_hbm, w_ref), (mask_hbm.at[pl.ds(mask_row, 8)], mask_ref), (ts_hbm, ts_ref),
        (gate_hbm, gate_v), (tok_hbm, tok_ref), (bias_hbm, bias_ref)))]
    for load in loads:
        load.start()

    barrier = pltpu.get_barrier_semaphore()
    far_z = jnp.where(c == 0, z + 2, z + 14)
    from_z = jnp.where(c == 0, z + 14, z + 2)
    peers = [f(d) for f in (zpeer, ypeer, xpeer) for d in (1, 2, 3)]
    peers += [at_z(z + 1, c), at_z(z + 15, c), at_z(far_z, c), at_z(from_z, c)]
    for dev in peers:
        pl.semaphore_signal(barrier, inc=1, device_id=dev, device_id_type=MESH)

    @pl.when(p > 0)
    def _():
        pl.semaphore_signal(barrier, inc=1, device_id=(seq - 1, head), device_id_type=MESH)

    @pl.when(p < 7)
    def _():
        pl.semaphore_signal(barrier, inc=1, device_id=(seq + 1, head), device_id_type=MESH)

    loads[0].wait()
    for g in range(4):
        first = (GROUP * g) // TILE
        off = GROUP * g - first * TILE
        tiles = -(-(off + GROUP) // TILE)
        piece = qkv_ref[:, first * TILE:(first + tiles) * TILE].astype(F32)
        starts = [off + 3 * HD * i for i in range(4)]
        cols = jnp.concatenate(
            [piece[:, a + HD:a + 3 * HD] for a in starts] + [piece[:, a:a + HD] for a in starts]
            + [jnp.zeros((piece.shape[0], GPAD - GROUP), F32)], axis=1)
        zsa[g] = cols[:, :CUT].astype(BF16)
        zsb[g] = cols[:, CUT:].astype(BF16)

    count = 13 + jnp.where(p > 0, 1, 0) + jnp.where(p < 7, 1, 0)
    pl.semaphore_wait(barrier, count)

    def start_z(src, dst, base):
        copies = []
        for d in (2, 1, 3):
            zc = remote(src.at[lax.rem(zh + d, 4)], dst.at[zh], base + d - 1, zpeer(d))
            zc.start()
            copies.append(zc)
        dst[zh] = src[zh]
        return copies

    za = start_z(zsa, zra, ZA)

    loads[1].wait()
    wf[COLS:48, :] = jnp.zeros((48 - COLS, wf.shape[1]), F32)
    wf[0:COLS, :] = w_ref[...].astype(F32)
    wide = wf[...]
    lane = lax.broadcasted_iota(jnp.int32, (48, 384), 1)
    shard = jnp.zeros((48, 384), F32)
    for g in range(4):
        turned = pltpu.roll(wide, lax.rem(wf.shape[1] + 80 * g - (g * 4 + y) * HD, wf.shape[1]), 1)[:, 0:384]
        shard = jnp.where((lane >= 80 * g) & (lane < 80 * g + HD), turned, shard)
    wall[c, x, zl] = shard.astype(BF16)
    own_shard = wall.at[c, x, zl]
    wz = [remote(own_shard, own_shard, WZ, at_z(z + 1, c)),
          remote(own_shard, own_shard, WZ + 1, at_z(z + 15, c)),
          remote(own_shard, own_shard, WZ + 2, at_z(far_z, c))]

    for f in range(4):
        kvbuf[f, KV:KVR, :] = jnp.ones((KVR - KV, 3 * BLOCK), BF16)

    @pl.when(p == 0)
    def _():
        for f in range(4):
            kvbuf[f, 0:KV, 0:BLOCK] = jnp.zeros((KV, BLOCK), BF16)

    @pl.when(p == 7)
    def _():
        for f in range(4):
            kvbuf[f, 0:KV, 2 * BLOCK:3 * BLOCK] = jnp.zeros((KV, BLOCK), BF16)

    for load in loads[2:]:
        load.wait()
    step = ts_ref[x]
    one_hot = (lax.broadcasted_iota(jnp.int32, (16, 1000), 1) == step).astype(F32).astype(BF16)
    gate_row[...] = jnp.dot(one_hot, gate_v[...], preferred_element_type=F32)

    for zc in za:
        zc.wait_send()
    zb = start_z(zsb, zrb, ZB)
    for zc in za:
        zc.wait_recv()

    for j in range(CUT // TILE):
        turn = zra[:, :, TILE * j:TILE * (j + 1)].reshape(TILE, TILE).astype(F32)
        zt[TILE * j:TILE * (j + 1), :] = jnp.transpose(turn)
    for g in range(4):
        ykv[g] = zt[KV * g:KV * (g + 1), :].astype(BF16)

    tiles_of = [y, lax.rem(y + 3, 4), lax.rem(y + 1, 4), lax.rem(y + 2, 4)]
    lanes_of = [pl.ds(pl.multiple_of(BLOCK + t * TILE, TILE), TILE) for t in tiles_of]
    ycopies = []
    for d in ORDER:
        yc = remote(ykv.at[lax.rem(y + d, 4)], kvbuf.at[x, 0:KV, lanes_of[0]], YK + d - 1, ypeer(d))
        yc.start()
        ycopies.append(yc)
    kvbuf[x, 0:KV, lanes_of[0]] = ykv[y]
    for w in wz:
        w.start()

    xcopies = {}
    for k in range(4):
        if k:
            ycopies[k - 1].wait()
        for d in ORDER:
            ref = kvbuf.at[x, 0:KV, lanes_of[k]]
            xcopies[d, k] = remote(ref, ref, X0 + 4 * (d - 1) + k, xpeer(d))
            xcopies[d, k].start()

    frames = (x, x - 1, x + 1)
    lives = (x >= 0, x > 0, x < 3)
    up, down = p < 7, p > 0

    def own_side(side):
        src = kvbuf.at[x, 0:KV, BLOCK:2 * BLOCK]
        if side == 0:
            return remote(src, kvbuf.at[x, 0:KV, 0:BLOCK], PO, (seq + 1, head))
        return remote(src, kvbuf.at[x, 0:KV, 2 * BLOCK:3 * BLOCK], PO + 1, (seq - 1, head))

    def pass_on(side, rel, k):
        src = kvbuf.at[frames[rel], 0:KV, lanes_of[k]]
        shift = -BLOCK if side == 0 else BLOCK
        lanes = pl.ds(pl.multiple_of(BLOCK + shift + tiles_of[k] * TILE, TILE), TILE)
        return remote(src, kvbuf.at[frames[rel], 0:KV, lanes], PF + (side * 2 + rel - 1) * 4 + k,
                      (seq + 1 - 2 * side, head))

    @pl.when(up)
    def _():
        own_side(0).start()

    @pl.when(down)
    def _():
        own_side(1).start()

    for zc in zb:
        zc.wait()
    for j in range((GPAD - CUT) // TILE):
        turn = zrb[:, :, TILE * j:TILE * (j + 1)].reshape(TILE, TILE).astype(F32)
        zt[CUT + TILE * j:CUT + TILE * (j + 1), :] = jnp.transpose(turn)
    for g in range(4):
        row = 4 * KV + HD * g
        yq[g] = jnp.concatenate([zt[row:row + HD, :], jnp.zeros((8, TILE), F32)], axis=0).astype(BF16)
    qcopies = []
    for d in ORDER:
        qc = remote(yq.at[lax.rem(y + d, 4)], qbuf.at[y], YQ + d - 1, ypeer(d))
        qc.start()
        qcopies.append(qc)
    qbuf[y] = yq[y]

    for w in wz:
        w.wait()
    group = wall.at[c, x]
    wx = {d: remote(group, group, WX + d - 1, xpeer(d)) for d in ORDER}
    for d in ORDER:
        wx[d].start()
    other = (seq + 1 - 2 * c, head)
    wc = [remote(group, group, WC, other)]
    wc[0].start()

    for qc in qcopies:
        qc.wait()
    for a in range(4):
        padded = jnp.concatenate([qbuf[a].astype(F32), jnp.zeros((48, TILE), F32)], axis=0)
        qs[a] = jnp.transpose(padded).astype(BF16)

    def attend(frame, tiles, first):
        @pl.loop(0, 4, unroll=True)
        def _(a):
            lead = 4 if tiles == 9 else 0
            base = a + 4 - lead
            lanes = pl.ds(pl.multiple_of(base * TILE, TILE), tiles * TILE)
            q = qs[a]
            s = jnp.dot(q, kvbuf[frame, 0:TILE, lanes], preferred_element_type=F32)
            top = None
            pens = []
            for t in range(tiles):
                spot = 4 * p + a - lead + t
                inside = (spot >= 0) & (spot < 32)
                live = mask_ref[4 * lax.rem(seq, 2) + a, frame * 32 + jnp.clip(spot, 0, 31)]
                pen = jnp.where(inside, jnp.where(live > 0, 0.0, FAR), FAR).astype(F32)
                pens.append(pen)
                val = s[:, t * TILE:(t + 1) * TILE] - pen
                top = val if top is None else jnp.maximum(top, val)
            m = jnp.max(top, axis=1, keepdims=True)
            if not first:
                old = mrun[a][:, 0:1]
                m = jnp.maximum(m, old)
            mc = m * C_EXP
            weights = jnp.concatenate(
                [jnp.exp2(s[:, t * TILE:(t + 1) * TILE] * C_EXP - (mc + pens[t])).astype(BF16)
                 for t in range(tiles)], axis=1)
            got = lax.dot_general(weights, kvbuf[frame, :, lanes], (((1,), (1,)), ((), ())),
                                  preferred_element_type=F32)
            if first:
                acc[a, :, 0:KVR] = got
            else:
                acc[a, :, 0:KVR] = acc[a, :, 0:KVR] * jnp.exp2((old - m) * C_EXP) + got
            mrun[a] = jnp.broadcast_to(m, (TILE, TILE))

    for k in range(4):
        for rel, d in ((1, 1), (2, 3)):
            xcopies[d, k].wait_recv()
            for side, gate_on in ((0, up), (1, down)):
                @pl.when(lives[rel] & gate_on)
                def _():
                    pass_on(side, rel, k).start()

    @pl.when(down)
    def _():
        own_side(0).wait_recv()

    @pl.when(up)
    def _():
        own_side(1).wait_recv()

    attend(x, 9, True)

    for k in range(4):
        xcopies[2, k].wait_recv()
    attend(lax.rem(x + 2, 4), 1, False)

    def passed(rel):
        for side, gate_on in ((0, down), (1, up)):
            @pl.when(lives[rel] & gate_on)
            def _():
                for k in range(4):
                    pass_on(side, rel, k).wait_recv()

    passed(1)

    @pl.when(x > 0)
    def _():
        attend(x - 1, 9, False)

    @pl.when(x == 0)
    def _():
        attend(3, 1, False)

    passed(2)

    @pl.when(x < 3)
    def _():
        attend(x + 1, 9, False)

    @pl.when(x == 3)
    def _():
        attend(0, 1, False)

    def finished(g):
        rows = acc[:, pl.ds(pl.multiple_of(32 * g, 32), 32), :].reshape(TILE, 2 * TILE)
        low = jnp.transpose(rows[:, 0:TILE])
        high = jnp.transpose(rows[:, TILE:2 * TILE])
        total = high[KV - TILE:KV - TILE + 1]
        feats = jnp.concatenate([low[HD:TILE], high[0:KV - TILE]], axis=0) / total
        return jnp.concatenate([feats, jnp.zeros((8, TILE), F32)], axis=0).astype(BF16)

    bcopies = []
    for d in (2, 1, 3):
        dest = lax.rem(zh + d, 4)
        bsend[d] = finished(dest)
        bc = remote(bsend.at[d], brecv.at[zh], B0 + d - 1, zpeer(d))
        bc.start()
        bcopies.append(bc)
    brecv[zh] = finished(zh)

    for n, d in enumerate(ORDER):
        wx[d].wait()
        got_x = wall.at[c, lax.rem(x + 4 - d, 4)]
        wc.append(remote(got_x, got_x, WC + 1 + n, other))
        wc[-1].start()
    for n, d in enumerate((0,) + ORDER):
        wc[n].wait()
        frm = lax.rem(x + 4 - d, 4)
        for s in range(8):
            piece = wall[s % 2, frm, s // 2]
            wfull[COLS * s:COLS * (s + 1), :] = piece[0:COLS].astype(F32)
        wt[pl.ds(pl.multiple_of(288 * frm, 32), 288), :] = wfull[...].astype(BF16)

    for bc in bcopies:
        bc.wait()

    feats = jnp.concatenate(
        [brecv[...].reshape(320, TILE).astype(F32), jnp.zeros((64, TILE), F32)], axis=0)
    att = jnp.concatenate(
        [jnp.transpose(feats[TILE * j:TILE * (j + 1)]) for j in range(3)], axis=1).astype(BF16)
    rcopies = []
    for j in range(3):
        res = lax.dot_general(att, wt[384 * j:384 * (j + 1)], (((1,), (1,)), ((), ())),
                              preferred_element_type=F32)
        part[j] = res
        for g in range(4):
            psend[j, g] = res[32 * g:32 * (g + 1)].astype(BF16)
        for d in (2, 1, 3):
            rc = remote(psend.at[j, lax.rem(y + d, 4)], precv.at[j, d - 1], R0 + 3 * j + d - 1, ypeer(d))
            rc.start()
            rcopies.append(rc)

    for j in range(3):
        for rc in rcopies[3 * j:3 * j + 3]:
            rc.wait()
        cols = slice(384 * j, 384 * (j + 1))
        proj = part[j, pl.ds(pl.multiple_of(32 * y, 32), 32), :] + bias_ref[cols].reshape(1, -1)
        for d in range(3):
            proj = proj + precv[j, d].astype(F32)
        out_ref[:, cols] = (tok_ref[:, cols].astype(F32) + gate_row[0:1, cols] * proj).astype(BF16)

    for copy in xcopies.values():
        copy.wait_send()
    for side, gate_on in ((0, up), (1, down)):
        @pl.when(gate_on)
        def _():
            own_side(side).wait_send()

        for rel in (1, 2):
            @pl.when(lives[rel] & gate_on)
            def _():
                for k in range(4):
                    pass_on(side, rel, k).wait_send()


def shards(tokens, qkv, out_weight, out_bias, gate_table, timesteps, tile_mask):
    d = tokens.shape[1]
    vm = pl.BlockSpec(memory_space=pltpu.VMEM)
    hbm = pl.BlockSpec(memory_space=pltpu.HBM)
    return pl.pallas_call(
        body,
        out_shape=jax.ShapeDtypeStruct(tokens.shape, BF16),
        in_specs=[hbm] * 7,
        out_specs=vm,
        scratch_shapes=[
            pltpu.VMEM(tokens.shape, BF16),
            pltpu.VMEM(qkv.shape, BF16),
            pltpu.VMEM(out_weight.shape[::-1], BF16),
            pltpu.VMEM((d,), F32),
            pltpu.SMEM(timesteps.shape, jnp.int32),
            pltpu.SMEM((8, tile_mask.shape[1]), jnp.int32),
            pltpu.VMEM((4, 32, CUT), BF16),
            pltpu.VMEM((4, 32, GPAD - CUT), BF16),
            pltpu.VMEM((4, 32, CUT), BF16),
            pltpu.VMEM((4, 32, GPAD - CUT), BF16),
            pltpu.VMEM((GPAD, TILE), F32),
            pltpu.VMEM((4, KV, TILE), BF16),
            pltpu.VMEM((4, 80, TILE), BF16),
            pltpu.VMEM((4, 80, TILE), BF16),
            pltpu.VMEM((4, TILE, TILE), BF16),
            pltpu.VMEM((4, KVR, 3 * BLOCK), BF16),
            pltpu.VMEM((4, TILE, 2 * TILE), F32),
            pltpu.VMEM((4, TILE, TILE), F32),
            pltpu.VMEM((4, 80, TILE), BF16),
            pltpu.VMEM((4, 80, TILE), BF16),
            pltpu.VMEM((48, d), F32),
            pltpu.VMEM((2, 4, 4, 48, 384), BF16),
            pltpu.VMEM((288, 384), F32),
            pltpu.VMEM((d, 384), BF16),
            pltpu.VMEM((3, TILE, 384), F32),
            pltpu.VMEM((3, 4, 32, 384), BF16),
            pltpu.VMEM((3, 3, 32, 384), BF16),
            pltpu.VMEM(gate_table.shape, BF16),
            pltpu.VMEM((16, d), F32),
            pltpu.SemaphoreType.DMA((NSEM,)),
            pltpu.SemaphoreType.DMA((NSEM,)),
            pltpu.SemaphoreType.DMA((7,)),
        ],
        compiler_params=pltpu.CompilerParams(
            collective_id=0, has_side_effects=True, vmem_limit_bytes=63 * 1024 * 1024),
    )(tokens, qkv, out_weight.T, out_bias, gate_table, timesteps, tile_mask)


def solution(mesh):
    return jax.shard_map(
        shards,
        mesh=mesh,
        in_specs=(
            P(("seq", "head"), None),
            P(("seq", "head"), None),
            P(None, "seq"),
            P(),
            P(),
            P(),
            P(),
        ),
        out_specs=P(("seq", "head"), None),
        check_vma=False,
    )
```

time: 72.6 us -> 61.2 us (0.84)
  the two profiles are of different devices: /device:TPU:67 before, /device:TPU:35 now
where the time goes in v2:
time: 61.2 us; the launch traced here: 61 us
  Pallas kernels  59.5 us (97%)
  local copies, waits for them, and re-layouts  1.52 us (2%)
    pallas_call x1, Pallas kernels, shards(): pl.pallas_call(body, out_shape=jax.ShapeDtypeStruct(tokens.shape, BF16),...  59.5 us
    unnamed x1, local copies, waits for them, and re-layouts  1.52 us

profile of v2, /device:TPU:35, one launch (start us, length us, event | category | flops | bytes accessed | tf_op | source)
XLA Modules:
  0.0 61.0 jit_solution(137311430528612349)
XLA Ops:
  0.0 59.5 %shard_map.73 = bf16[32,1152]{1,0:T(8,128)(2,1)} custom-call(bf16[32,1152]{1,0:T(8,128)(2,1)} %tok_hbm.1, bf16[32,3456]{1,0:T(8,128)(2,1)} %qkv_hbm.1, bf16[36,1152]{1,0:T(8,128)(2,1)} %bitcast.1, f32[1152]{0:T(1024)} %bias_hbm.1, bf16[1000,1152]{1,0:T(8,128)(2,1)} %gate_hbm.1, s32[4]{0:T(128)} %ts_hbm.1, s32[128,128]{1,0:T(8,128)} %mask_hbm.1), custom_call_target="tpu_custom_call" | custom-call | tf_op jit(solution)/shard_map/pallas_call | solution.py:394
  59.5 1.5 %copy.9 = bf16[32,1152]{1,0:T(8,128)(2,1)} copy(bf16[32,1152]{1,0:T(8,128)(2,1)} %shard_map.73) | data formatting | bytes 147456

commit v3 on v2

--- a/solution.py
+++ b/solution.py
@@ -215,22 +215,6 @@
         qc.start()
         qcopies.append(qc)
     qbuf[y] = yq[y]
-
-    for w in wz:
-        w.wait()
-    group = wall.at[c, x]
-    wx = {d: remote(group, group, WX + d - 1, xpeer(d)) for d in ORDER}
-    for d in ORDER:
-        wx[d].start()
-    other = (seq + 1 - 2 * c, head)
-    wc = [remote(group, group, WC, other)]
-    wc[0].start()
-
-    for qc in qcopies:
-        qc.wait()
-    for a in range(4):
-        padded = jnp.concatenate([qbuf[a].astype(F32), jnp.zeros((48, TILE), F32)], axis=0)
-        qs[a] = jnp.transpose(padded).astype(BF16)
 
     def attend(frame, tiles, first):
         @pl.loop(0, 4, unroll=True)
@@ -273,6 +257,22 @@
                 @pl.when(lives[rel] & gate_on)
                 def _():
                     pass_on(side, rel, k).start()
+
+    for qc in qcopies:
+        qc.wait()
+    for a in range(4):
+        padded = jnp.concatenate([qbuf[a].astype(F32), jnp.zeros((48, TILE), F32)], axis=0)
+        qs[a] = jnp.transpose(padded).astype(BF16)
+
+    for w in wz:
+        w.wait()
+    group = wall.at[c, x]
+    wx = {d: remote(group, group, WX + d - 1, xpeer(d)) for d in ORDER}
+    for d in ORDER:
+        wx[d].start()
+    other = (seq + 1 - 2 * c, head)
+    wc = [remote(group, group, WC, other)]
+    wc[0].start()
 
     @pl.when(down)
     def _():
@@ -431,8 +431,9 @@
             pltpu.SemaphoreType.DMA((7,)),
         ],
         compiler_params=pltpu.CompilerParams(
-            collective_id=0, has_side_effects=True, vmem_limit_bytes=63 * 1024 * 1024),
-    )(tokens, qkv, out_weight.T, out_bias, gate_table, timesteps, tile_mask)
+            collective_id=0, has_side_effects=True, vmem_limit_bytes=40 * 1024 * 1024),
+    )(*[pltpu.with_memory_space_constraint(a, pltpu.HBM) for a in (
+        tokens, qkv, out_weight.T, out_bias, gate_table, timesteps, tile_mask)])
 
 
 def solution(mesh):

time: 61.2 us -> 57.7 us (0.943)
  the two profiles are of different devices: /device:TPU:35 before, /device:TPU:32 now
where the time goes in v3:
time: 57.7 us; the launch traced here: 57.6 us
  Pallas kernels  57 us (99%)
  local copies, waits for them, and re-layouts  0.64 us (1%)
    pallas_call x1, Pallas kernels, shards(): pl.pallas_call(body, out_shape=jax.ShapeDtypeStruct(tokens.shape, BF16),...  57 us

profile of v3, /device:TPU:32, one launch (start us, length us, event | category | flops | bytes accessed | tf_op | source)
XLA Modules:
  0.0 57.6 jit_solution(11170748561036695050)
XLA Ops:
  0.0 57.0 %shard_map.73 = bf16[32,1152]{1,0:T(8,128)(2,1)S(1)} custom-call(bf16[32,1152]{1,0:T(8,128)(2,1)} %tok_hbm.1, bf16[32,3456]{1,0:T(8,128)(2,1)} %qkv_hbm.1, bf16[36,1152]{1,0:T(8,128)(2,1)} %bitcast.1, f32[1152]{0:T(1024)} %bias_hbm.1, bf16[1000,1152]{1,0:T(8,128)(2,1)} %gate_hbm.1, s32[4]{0:T(128)} %ts_hbm.1, s32[128,128]{1,0:T(8,128)} %mask_hbm.1), custom_call_target="tpu_custom_call" | custom-call | tf_op jit(solution)/shard_map/pallas_call | solution.py:394
  57.0 0.6 %copy.9 = bf16[32,1152]{1,0:T(8,128)(2,1)} copy(bf16[32,1152]{1,0:T(8,128)(2,1)S(1)} %shard_map.73) | data formatting | bytes 147456

commit v4 on v3

--- a/solution.py
+++ b/solution.py
@@ -24,7 +24,7 @@
 FAR = 1e30
 C_EXP = HD ** (-0.5) * math.log2(math.e)
 
-ZA, ZB, YK, YQ, X0, PO, PF, WZ, WX, WC, B0, R0, NSEM = 0, 3, 6, 9, 12, 24, 26, 42, 45, 48, 52, 55, 64
+ZA, ZB, YK, YQ, X0, PF, WZ, WX, WC, B0, R0, NSEM = 0, 3, 6, 9, 12, 24, 48, 51, 54, 58, 61, 70
 ORDER = (1, 3, 2)
 
 
@@ -125,6 +125,8 @@
           remote(own_shard, own_shard, WZ + 1, at_z(z + 15, c)),
           remote(own_shard, own_shard, WZ + 2, at_z(far_z, c))]
 
+    for w in wz:
+        w.start()
     for f in range(4):
         kvbuf[f, KV:KVR, :] = jnp.ones((KVR - KV, 3 * BLOCK), BF16)
 
@@ -164,8 +166,23 @@
         yc.start()
         ycopies.append(yc)
     kvbuf[x, 0:KV, lanes_of[0]] = ykv[y]
-    for w in wz:
-        w.start()
+
+    frames = (x, x - 1, x + 1)
+    lives = (x >= 0, x > 0, x < 3)
+    up, down = p < 7, p > 0
+
+    def pass_on(side, rel, k):
+        src = kvbuf.at[frames[rel], 0:KV, lanes_of[k]]
+        shift = -BLOCK if side == 0 else BLOCK
+        lanes = pl.ds(pl.multiple_of(BLOCK + shift + tiles_of[k] * TILE, TILE), TILE)
+        return remote(src, kvbuf.at[frames[rel], 0:KV, lanes], PF + (side * 3 + rel) * 4 + k,
+                      (seq + 1 - 2 * side, head))
+
+    def pass_tile(rel, k):
+        for side, gate_on in ((0, up), (1, down)):
+            @pl.when(lives[rel] & gate_on)
+            def _():
+                pass_on(side, rel, k).start()
 
     xcopies = {}
     for k in range(4):
@@ -175,31 +192,7 @@
             ref = kvbuf.at[x, 0:KV, lanes_of[k]]
             xcopies[d, k] = remote(ref, ref, X0 + 4 * (d - 1) + k, xpeer(d))
             xcopies[d, k].start()
-
-    frames = (x, x - 1, x + 1)
-    lives = (x >= 0, x > 0, x < 3)
-    up, down = p < 7, p > 0
-
-    def own_side(side):
-        src = kvbuf.at[x, 0:KV, BLOCK:2 * BLOCK]
-        if side == 0:
-            return remote(src, kvbuf.at[x, 0:KV, 0:BLOCK], PO, (seq + 1, head))
-        return remote(src, kvbuf.at[x, 0:KV, 2 * BLOCK:3 * BLOCK], PO + 1, (seq - 1, head))
-
-    def pass_on(side, rel, k):
-        src = kvbuf.at[frames[rel], 0:KV, lanes_of[k]]
-        shift = -BLOCK if side == 0 else BLOCK
-        lanes = pl.ds(pl.multiple_of(BLOCK + shift + tiles_of[k] * TILE, TILE), TILE)
-        return remote(src, kvbuf.at[frames[rel], 0:KV, lanes], PF + (side * 2 + rel - 1) * 4 + k,
-                      (seq + 1 - 2 * side, head))
-
-    @pl.when(up)
-    def _():
-        own_side(0).start()
-
-    @pl.when(down)
-    def _():
-        own_side(1).start()
+        pass_tile(0, k)
 
     for zc in zb:
         zc.wait()
@@ -253,10 +246,7 @@
     for k in range(4):
         for rel, d in ((1, 1), (2, 3)):
             xcopies[d, k].wait_recv()
-            for side, gate_on in ((0, up), (1, down)):
-                @pl.when(lives[rel] & gate_on)
-                def _():
-                    pass_on(side, rel, k).start()
+            pass_tile(rel, k)
 
     for qc in qcopies:
         qc.wait()
@@ -274,26 +264,20 @@
     wc = [remote(group, group, WC, other)]
     wc[0].start()
 
-    @pl.when(down)
-    def _():
-        own_side(0).wait_recv()
-
-    @pl.when(up)
-    def _():
-        own_side(1).wait_recv()
-
-    attend(x, 9, True)
-
-    for k in range(4):
-        xcopies[2, k].wait_recv()
-    attend(lax.rem(x + 2, 4), 1, False)
-
     def passed(rel):
         for side, gate_on in ((0, down), (1, up)):
             @pl.when(lives[rel] & gate_on)
             def _():
                 for k in range(4):
                     pass_on(side, rel, k).wait_recv()
+
+    passed(0)
+
+    attend(x, 9, True)
+
+    for k in range(4):
+        xcopies[2, k].wait_recv()
+    attend(lax.rem(x + 2, 4), 1, False)
 
     passed(1)
 
@@ -375,12 +359,8 @@
 
     for copy in xcopies.values():
         copy.wait_send()
-    for side, gate_on in ((0, up), (1, down)):
-        @pl.when(gate_on)
-        def _():
-            own_side(side).wait_send()
-
-        for rel in (1, 2):
+    for rel in range(3):
+        for side, gate_on in ((0, up), (1, down)):
             @pl.when(lives[rel] & gate_on)
             def _():
                 for k in range(4):

time: 57.7 us -> 57.3 us (level)
  the two profiles are of different devices: /device:TPU:32 before, /device:TPU:35 now
where the time goes in v4:
time: 57.3 us; the launch traced here: 57.2 us
  Pallas kernels  56.5 us (99%)
  local copies, waits for them, and re-layouts  0.64 us (1%)
    pallas_call x1, Pallas kernels, shards(): pl.pallas_call(body, out_shape=jax.ShapeDtypeStruct(tokens.shape, BF16),...  56.5 us

profile of v4, /device:TPU:35, one launch (start us, length us, event | category | flops | bytes accessed | tf_op | source)
XLA Modules:
  0.0 57.2 jit_solution(10575550794887951407)
XLA Ops:
  0.0 56.5 %shard_map.73 = bf16[32,1152]{1,0:T(8,128)(2,1)S(1)} custom-call(bf16[32,1152]{1,0:T(8,128)(2,1)} %tok_hbm.1, bf16[32,3456]{1,0:T(8,128)(2,1)} %qkv_hbm.1, bf16[36,1152]{1,0:T(8,128)(2,1)} %bitcast.1, f32[1152]{0:T(1024)} %bias_hbm.1, bf16[1000,1152]{1,0:T(8,128)(2,1)} %gate_hbm.1, s32[4]{0:T(128)} %ts_hbm.1, s32[128,128]{1,0:T(8,128)} %mask_hbm.1), custom_call_target="tpu_custom_call" | custom-call | tf_op jit(solution)/shard_map/pallas_call | solution.py:374
  56.5 0.6 %copy.9 = bf16[32,1152]{1,0:T(8,128)(2,1)} copy(bf16[32,1152]{1,0:T(8,128)(2,1)S(1)} %shard_map.73) | data formatting | bytes 147456

commit v5 on v4

--- a/solution.py
+++ b/solution.py
@@ -210,7 +210,7 @@
     qbuf[y] = yq[y]
 
     def attend(frame, tiles, first):
-        @pl.loop(0, 4, unroll=True)
+        @pl.loop(0, 4, unroll=2)
         def _(a):
             lead = 4 if tiles == 9 else 0
             base = a + 4 - lead

time: 57.3 us -> 57.2 us (level)
  no operation moved by 1% of the time
where the time goes in v5:
time: 57.2 us; the launch traced here: 57.1 us
  Pallas kernels  56.4 us (99%)
  local copies, waits for them, and re-layouts  0.64 us (1%)
    pallas_call x1, Pallas kernels, shards(): pl.pallas_call(body, out_shape=jax.ShapeDtypeStruct(tokens.shape, BF16),...  56.4 us

profile of v5, /device:TPU:35, one launch (start us, length us, event | category | flops | bytes accessed | tf_op | source)
XLA Modules:
  0.0 57.1 jit_solution(5432835378536350438)
XLA Ops:
  0.0 56.4 %shard_map.73 = bf16[32,1152]{1,0:T(8,128)(2,1)S(1)} custom-call(bf16[32,1152]{1,0:T(8,128)(2,1)} %tok_hbm.1, bf16[32,3456]{1,0:T(8,128)(2,1)} %qkv_hbm.1, bf16[36,1152]{1,0:T(8,128)(2,1)} %bitcast.1, f32[1152]{0:T(1024)} %bias_hbm.1, bf16[1000,1152]{1,0:T(8,128)(2,1)} %gate_hbm.1, s32[4]{0:T(128)} %ts_hbm.1, s32[128,128]{1,0:T(8,128)} %mask_hbm.1), custom_call_target="tpu_custom_call" | custom-call | tf_op jit(solution)/shard_map/pallas_call | solution.py:374
  56.4 0.6 %copy.9 = bf16[32,1152]{1,0:T(8,128)(2,1)} copy(bf16[32,1152]{1,0:T(8,128)(2,1)S(1)} %shard_map.73) | data formatting | bytes 147456

commit v6 on v5

--- a/solution.py
+++ b/solution.py
@@ -24,7 +24,7 @@
 FAR = 1e30
 C_EXP = HD ** (-0.5) * math.log2(math.e)
 
-ZA, ZB, YK, YQ, X0, PF, WZ, WX, WC, B0, R0, NSEM = 0, 3, 6, 9, 12, 24, 48, 51, 54, 58, 61, 70
+ZA, ZB, YK, YQ, X0, PF, WZ, WX, WC, B0, R0, NSEM = 0, 3, 6, 9, 12, 24, 48, 51, 54, 58, 61, 64
 ORDER = (1, 3, 2)
 
 
@@ -337,8 +337,8 @@
     att = jnp.concatenate(
         [jnp.transpose(feats[TILE * j:TILE * (j + 1)]) for j in range(3)], axis=1).astype(BF16)
     rcopies = []
-    for j in range(3):
-        res = lax.dot_general(att, wt[384 * j:384 * (j + 1)], (((1,), (1,)), ((), ())),
+    for j in range(1):
+        res = lax.dot_general(att, wt[1152 * j:1152 * (j + 1)], (((1,), (1,)), ((), ())),
                               preferred_element_type=F32)
         part[j] = res
         for g in range(4):
@@ -348,10 +348,10 @@
             rc.start()
             rcopies.append(rc)
 
-    for j in range(3):
+    for j in range(1):
         for rc in rcopies[3 * j:3 * j + 3]:
             rc.wait()
-        cols = slice(384 * j, 384 * (j + 1))
+        cols = slice(1152 * j, 1152 * (j + 1))
         proj = part[j, pl.ds(pl.multiple_of(32 * y, 32), 32), :] + bias_ref[cols].reshape(1, -1)
         for d in range(3):
             proj = proj + precv[j, d].astype(F32)
@@ -401,9 +401,9 @@
             pltpu.VMEM((2, 4, 4, 48, 384), BF16),
             pltpu.VMEM((288, 384), F32),
             pltpu.VMEM((d, 384), BF16),
-            pltpu.VMEM((3, TILE, 384), F32),
-            pltpu.VMEM((3, 4, 32, 384), BF16),
-            pltpu.VMEM((3, 3, 32, 384), BF16),
+            pltpu.VMEM((1, TILE, 1152), F32),
+            pltpu.VMEM((1, 4, 32, 1152), BF16),
+            pltpu.VMEM((1, 3, 32, 1152), BF16),
             pltpu.VMEM(gate_table.shape, BF16),
             pltpu.VMEM((16, d), F32),
             pltpu.SemaphoreType.DMA((NSEM,)),

time: 57.2 us -> 57.3 us (level)
  no operation moved by 1% of the time
where the time goes in v6:
time: 57.3 us; the launch traced here: 57.1 us
  Pallas kernels  56.5 us (99%)
  local copies, waits for them, and re-layouts  0.64 us (1%)
    pallas_call x1, Pallas kernels, shards(): pl.pallas_call(body, out_shape=jax.ShapeDtypeStruct(tokens.shape, BF16),...  56.5 us

profile of v6, /device:TPU:35, one launch (start us, length us, event | category | flops | bytes accessed | tf_op | source)
XLA Modules:
  0.0 57.1 jit_solution(4374847809770018339)
XLA Ops:
  0.0 56.5 %shard_map.73 = bf16[32,1152]{1,0:T(8,128)(2,1)S(1)} custom-call(bf16[32,1152]{1,0:T(8,128)(2,1)} %tok_hbm.1, bf16[32,3456]{1,0:T(8,128)(2,1)} %qkv_hbm.1, bf16[36,1152]{1,0:T(8,128)(2,1)} %bitcast.1, f32[1152]{0:T(1024)} %bias_hbm.1, bf16[1000,1152]{1,0:T(8,128)(2,1)} %gate_hbm.1, s32[4]{0:T(128)} %ts_hbm.1, s32[128,128]{1,0:T(8,128)} %mask_hbm.1), custom_call_target="tpu_custom_call" | custom-call | tf_op jit(solution)/shard_map/pallas_call | solution.py:374
  56.5 0.6 %copy.9 = bf16[32,1152]{1,0:T(8,128)(2,1)} copy(bf16[32,1152]{1,0:T(8,128)(2,1)S(1)} %shard_map.73) | data formatting | bytes 147456
